TPU v7x, 32 devices: a whole 2x2x4 slice. The times are simulated.
32 devices in a mesh: seq: 8 (over z, x), head: 4 (over y, core).
Axes of the slice: x: 2, y: 2, z: 4, core: 2. Of those that a mesh axis runs over, the one named last changes fastest.
Arguments:
- inputs: float32 [8192, 4096], P('seq', 'head'), may hold values from -6 to 6
- cotangent: float32 [8192, 4096], P('seq', 'head'), may hold values from -1.5 to 1.5
- b_proj: float32 [8192, 128], P('seq'), may hold values from -1.8 to 1.8
- c_proj: float32 [8192, 128], P('seq'), may hold values from -1.8 to 1.8
- decay_rate: float32 [64], P('head'), may hold values from 1e-06 to 0.0001
- level_weight: float32 [8, 64, 8192], P(None, 'head', 'seq'), may hold values from 0 to 2, as said below
- starts: int32 [128], P('seq'), may hold values from 0 to 1, as said below
Outputs:
- grad_x: float32 [8192, 4096], P('seq', 'head')
- grad_b: float32 [8192, 128], P(('seq', 'head'))
- grad_c: float32 [8192, 128], P(('seq', 'head'))
- grad_level: float32 [8, 64, 8192], P(None, 'head', 'seq')
Inputs may be any that keep to these rules, and one draw needn't show every extreme that they name: `starts`: exactly two of the 128 stretches carry 1. `level_weight`: positive.
All inputs are finite; a program needn't handle non-finite values.
Results may differ from a plain program's by a relative error of at most 0.0001.
Values sent between devices are 32-bit elements; how exact they have to be, the bound alone decides.
No kernel may reach another device: no remote copies, remote signals or barrier semaphores. Data moves between devices by JAX's collectives and lax.ppermute only.
A program may use at most 128 MiB of HBM per device.

v0:
```python
import jax
import jax.numpy as jnp
from jax import lax
from jax.sharding import PartitionSpec as P

STRETCH = 64


def from_partner(x, axis, apart):
    return lax.ppermute(x, axis, [(i, i ^ 1 << apart) for i in range(lax.axis_size(axis))])


def local(inputs, cotangent, b_proj, c_proj, decay_rate, level_weight, starts):
    highest = lax.Precision.HIGHEST
    rows_dev = inputs.shape[0]
    head_count = decay_rate.shape[0]
    width = inputs.shape[1] // head_count
    seq_count = lax.axis_size("seq")
    seq_bits = seq_count.bit_length() - 1
    stretch_count = rows_dev // STRETCH
    stretch_bits = stretch_count.bit_length() - 1
    seq_index = lax.axis_index("seq")
    level_count = level_weight.shape[0]
    level_scale = (STRETCH * 2.0 ** jnp.arange(level_count, dtype=jnp.float32)) ** (-0.5)
    level_vals = level_weight * level_scale[:, None, None]
    position = (seq_index * rows_dev + jnp.arange(rows_dev) - seq_count * rows_dev // 2).astype(
        jnp.float32
    )
    decay_query = jnp.exp(-decay_rate[:, None] * position[None, :])
    decay_key = jnp.exp(decay_rate[:, None] * position[None, :])
    open_flag = 1.0 - starts.astype(jnp.float32)
    prefix_open = jnp.cumprod(open_flag)
    suffix_open = jnp.concatenate(
        [jnp.cumprod(open_flag[::-1])[::-1][1:], jnp.ones((1,), jnp.float32)]
    )
    device_clean = prefix_open[stretch_count - 1]
    prefix_rows = jnp.repeat(prefix_open, STRETCH)
    suffix_rows = jnp.repeat(suffix_open, STRETCH)
    x_heads = inputs.reshape(rows_dev, head_count, width)
    cot_heads = cotangent.reshape(rows_dev, head_count, width)
    key_weight = decay_key * suffix_rows[None, :]
    tail_total = jnp.einsum(
        "sn,shp->hnp", b_proj, x_heads * key_weight.T[:, :, None], precision=highest
    )
    query_weight = decay_query * prefix_rows[None, :]
    cross_level = level_vals[stretch_bits + 1 :]
    head_totals = jnp.einsum(
        "tn,kthp->khnp",
        c_proj,
        cot_heads[None] * jnp.transpose(cross_level * query_weight[None], (0, 2, 1))[..., None],
        precision=highest,
    )
    own_clean = device_clean
    before_clean = jnp.float32(1.0)
    after_clean = jnp.float32(1.0)
    carried = head_totals
    fwd_gates = []
    rev_totals = []
    rev_gates = []
    upper_list = []
    for level_bit in range(seq_bits):
        upper_half = (seq_index // 2**level_bit % 2).astype(jnp.float32)
        upper_list.append(upper_half)
        payload = (carried, own_clean)
        received = from_partner((payload[0], payload[1]), "seq", level_bit)
        far_heads = received[0]
        far_clean = received[len(received) - 1]
        rev_totals.append((1.0 - upper_half) * far_heads[0])
        rev_gates.append((1.0 - upper_half) * after_clean)
        fwd_gates.append(upper_half * before_clean)
        carried = upper_half * (far_heads[1:] + far_clean * carried[1:]) + (1.0 - upper_half) * (
            carried[1:] + own_clean * far_heads[1:]
        )
        before_clean = upper_half * far_clean * before_clean + (1.0 - upper_half) * before_clean
        after_clean = (1.0 - upper_half) * far_clean * after_clean + upper_half * after_clean
        own_clean = own_clean * far_clean
    all_tail, all_clean = (
        lax.all_gather(tail_total[None], "seq", axis=0, tiled=True),
        lax.all_gather(device_clean[None], "seq", axis=0, tiled=True),
    )
    zero_count = jnp.cumsum(1.0 - all_clean)
    device_ids = jnp.arange(seq_count)
    weight_rows = []
    for level_bit in range(seq_bits):
        stride = 2**level_bit
        block_base = (seq_index // stride ^ 1) * stride
        block_end = block_base + stride - 1
        end_count = jnp.sum(jnp.where(device_ids == block_end, zero_count, 0.0))
        inside = (
            (device_ids >= block_base) & (device_ids <= block_end) & (end_count - zero_count == 0.0)
        )
        weight_rows.append(jnp.where(inside, 1.0, 0.0) * upper_list[level_bit])
    fwd_state = jnp.einsum("km,mhnp->khnp", jnp.stack(weight_rows), all_tail, precision=highest)
    rev_state = jnp.stack(rev_totals)
    fwd_gate = jnp.stack(fwd_gates)
    rev_gate = jnp.stack(rev_gates)
    query_gate = fwd_gate[:, None, None] * query_weight[None]
    lam_query = cross_level * query_gate
    weighted_cot = cot_heads[None] * jnp.transpose(lam_query, (0, 2, 1))[..., None]
    grad_c_cross = jnp.einsum("kthp,khnp->tn", weighted_cot, fwd_state, precision=highest)
    projected = jnp.einsum("tn,khnp->kthp", c_proj, fwd_state, precision=highest)
    grad_lam_cross = query_gate * jnp.transpose(
        jnp.sum(projected * cot_heads[None], axis=-1), (0, 2, 1)
    )
    rev_combined = jnp.einsum("k,khnp->hnp", rev_gate, rev_state, precision=highest)
    key_rows = key_weight.T[:, :, None]
    grad_x_cross = jnp.einsum("sn,hnp->shp", b_proj, rev_combined, precision=highest) * key_rows
    grad_b_cross = jnp.einsum("shp,hnp->sn", x_heads * key_rows, rev_combined, precision=highest)
    local_stretch = jnp.arange(rows_dev) // STRETCH
    differ = local_stretch[:, None] ^ local_stretch[None, :]
    local_level = jnp.zeros_like(differ)
    for level_bit in range(stretch_bits):
        local_level = local_level + (differ >= 2**level_bit).astype(jnp.int32)
    local_doc = jnp.cumsum(starts)[local_stretch]
    row_ids = jnp.arange(rows_dev)
    valid = (row_ids[:, None] >= row_ids[None, :]) & (local_doc[:, None] == local_doc[None, :])
    scores = jnp.dot(c_proj, b_proj.T, precision=highest)

    def head_step(mixed_sum, pieces):
        x_one, cot_one, query_decay, key_decay, lam_one = pieces
        decayed = jnp.where(valid, query_decay[:, None] * key_decay[None, :], 0.0)
        lam_pair = jnp.zeros((rows_dev, rows_dev), jnp.float32)
        for level in range(stretch_bits + 1):
            lam_pair = jnp.where(local_level == level, lam_one[level][:, None], lam_pair)
        inner = jnp.dot(cot_one, x_one.T, precision=highest)
        kernel = decayed * lam_pair
        weighted = kernel * scores
        plain = decayed * scores * inner
        grad_x_one = jnp.dot(weighted.T, cot_one, precision=highest)
        grad_lam_one = jnp.stack(
            [
                jnp.sum(jnp.where(local_level == level, plain, 0.0), axis=1)
                for level in range(stretch_bits + 1)
            ]
        )
        return (mixed_sum + kernel * inner, (grad_x_one, grad_lam_one))

    pieces = (
        jnp.transpose(x_heads, (1, 0, 2)),
        jnp.transpose(cot_heads, (1, 0, 2)),
        decay_query,
        decay_key,
        jnp.transpose(level_vals[: stretch_bits + 1], (1, 0, 2)),
    )
    mixed_total, (grad_x_local, grad_lam_local) = lax.scan(
        head_step, jnp.zeros((rows_dev, rows_dev), jnp.float32), pieces
    )
    local_c = grad_c_cross + jnp.dot(mixed_total, b_proj, precision=highest)
    local_b = grad_b_cross + jnp.dot(mixed_total.T, c_proj, precision=highest)
    grad_x = (jnp.transpose(grad_x_local, (1, 0, 2)) + grad_x_cross).reshape(
        rows_dev, head_count * width
    )
    grad_level = (
        jnp.concatenate([jnp.transpose(grad_lam_local, (1, 0, 2)), grad_lam_cross], 0)
        * level_scale[:, None, None]
    )
    grad_b, grad_c = (
        lax.psum_scatter(local_b, "head", scatter_dimension=0, tiled=True),
        lax.psum_scatter(local_c, "head", scatter_dimension=0, tiled=True),
    )
    return (grad_x, grad_b, grad_c, grad_level)


def solution(mesh):
    return jax.shard_map(
        local,
        mesh=mesh,
        in_specs=(
            P("seq", "head"),
            P("seq", "head"),
            P("seq", None),
            P("seq", None),
            P("head"),
            P(None, "head", "seq"),
            P("seq"),
        ),
        out_specs=(
            P("seq", "head"),
            P(("seq", "head"), None),
            P(("seq", "head"), None),
            P(None, "head", "seq"),
        ),
        check_vma=False,
    )
```

profile of v0, /device:TPU:0, one launch (start us, length us, event | category | flops | bytes accessed | tf_op | source)
XLA Modules:
  0.0 729.3 jit_solution(16242255150893106869)
XLA Ops:
  25.5 21.2 %all-reduce = f32[8]{0:T(128)S(1)} all-reduce(f32[8]{0:T(128)S(1)} %bitcast_dynamic-update-slice_fusion), channel_id=2, replica_groups=mesh['seq'=8,'head'=4] {'seq'}, use_global_device_ids=true, to_apply=%add | all-reduce | flops 8 | bytes 64
  62.4 33.9 %all-gather.4.cloned.1.call-done = f32[128,128,64]{1,2,0:T(8,128)} async-done(((f32[16,128,64]{1,2,0:T(8,128)}), f32[128,128,64]{1,2,0:T(8,128)}) %all-gather.4.cloned.1.call-update) | async-done | bytes 4194320 | tf_op jit(solution)/shard_map/all_gather | solution.py:78
  104.6 11.6 %fusion.30 = f32[3,1024,16]{1,2,0:T(8,128)S(1)} fusion(f32[1024,16,64]{0,2,1:T(8,128)S(1)} %bitcast.202, f32[3,16,128,64]{2,0,3,1:T(4,128)S(1)} %fusion.38, f32[1024,128]{1,0:T(8,128)S(1)} %copy-done.5), kind=kOutput, calls=%fused_computation.50 | convolution fusion | flops 4838080512 | bytes 6488064 | tf_op jit(solution)/shard_map/tn,khnp->kthp/dot_general | solution.py:101
  118.0 11.2 %fusion.50 = f32[3,16,128,64]{2,3,1,0:T(8,128)} fusion(f32[3,1024,16]{1,2,0:T(8,128)S(1)} %get-tuple-element.287, f32[1024,16,64]{0,2,1:T(8,128)S(1)} %bitcast.203, f32[1024,128]{1,0:T(8,128)S(1)} %copy-done.5), kind=kOutput, calls=%fused_computation.73 | convolution fusion | flops 4834983936 | bytes 6488064 | tf_op jit(solution)/shard_map/tn,kthp->khnp/dot_general | solution.py:47
  147.3 17.1 %collective-permute-done.2 = f32[3,16,128,64]{2,3,1,0:T(8,128)} collective-permute-done((f32[3,16,128,64]{2,3,1,0:T(8,128)}, f32[3,16,128,64]{2,3,1,0:T(8,128)}, u32[]{:S(2)}, u32[]{:S(2)}) %collective-permute-start.2) | collective-permute-done | bytes 1572896 | tf_op jit(solution)/shard_map/ppermute | solution.py:10
  169.6 465.9 %while.16 = (s32[]{:T(128)}, f32[1024,1024]{0,1:T(8,128)}, f32[16,1024,64]{1,2,0:T(8,128)}, f32[16,5,1024]{2,0,1:T(8,128)}, f32[16,1024]{1,0:T(8,128)}, /*index=...) while((s32[]{:T(128)}, f32[1024,1024]{0,1:T(8,128)}, ...), condition=%wide.region_7.8_spmd.clone.clone, body=%wide.region_1.0_spmd.clone.clone.sunk | while | flops 1703930880 | bytes 43289372 | solution.py:145
  171.4 11.7 %multiply_multiply_fusion.4 = (f32[1024,1024]{0,1:T(8,128)S(1)}, f32[1024,1024]{0,1:T(8,128)}) fusion(f32[1024,1024]{0,1:T(8,128)} %get-tuple-element.459, s32[1024]{0:T(1024)S(1)} %get-tuple-element.460, f32[1024]{0:T(1024)S(1)} %bitcast.219, f32[1024]{0:T(1024)S(1)} %bitcast.221, f32[1024]{0:T(1024)S(1)} %bitcast.231, f32[1024]{0:T(1024)S(1)} %bitcast.225, ...), kind=kOutput, calls=%fused_computation.14.clone.1 | convolution fusion | flops 839909376 | bytes 17348096 | tf_op jit(solution)/shard_map/while/body/eval_jaxpr/dot_general | solution.py:125
  200.1 12.1 %multiply_multiply_fusion.4 = (f32[1024,1024]{0,1:T(8,128)S(1)}, f32[1024,1024]{0,1:T(8,128)}) fusion(f32[1024,1024]{0,1:T(8,128)} %get-tuple-element.459, s32[1024]{0:T(1024)S(1)} %get-tuple-element.460, f32[1024]{0:T(1024)S(1)} %bitcast.219, f32[1024]{0:T(1024)S(1)} %bitcast.221, f32[1024]{0:T(1024)S(1)} %bitcast.231, f32[1024]{0:T(1024)S(1)} %bitcast.225, ...), kind=kOutput, calls=%fused_computation.14.clone.1 | convolution fusion | flops 839909376 | bytes 17348096 | tf_op jit(solution)/shard_map/while/body/eval_jaxpr/dot_general | solution.py:125
  229.2 12.1 %multiply_multiply_fusion.4 = (f32[1024,1024]{0,1:T(8,128)S(1)}, f32[1024,1024]{0,1:T(8,128)}) fusion(f32[1024,1024]{0,1:T(8,128)} %get-tuple-element.459, s32[1024]{0:T(1024)S(1)} %get-tuple-element.460, f32[1024]{0:T(1024)S(1)} %bitcast.219, f32[1024]{0:T(1024)S(1)} %bitcast.221, f32[1024]{0:T(1024)S(1)} %bitcast.231, f32[1024]{0:T(1024)S(1)} %bitcast.225, ...), kind=kOutput, calls=%fused_computation.14.clone.1 | convolution fusion | flops 839909376 | bytes 17348096 | tf_op jit(solution)/shard_map/while/body/eval_jaxpr/dot_general | solution.py:125
  258.3 12.1 %multiply_multiply_fusion.4 = (f32[1024,1024]{0,1:T(8,128)S(1)}, f32[1024,1024]{0,1:T(8,128)}) fusion(f32[1024,1024]{0,1:T(8,128)} %get-tuple-element.459, s32[1024]{0:T(1024)S(1)} %get-tuple-element.460, f32[1024]{0:T(1024)S(1)} %bitcast.219, f32[1024]{0:T(1024)S(1)} %bitcast.221, f32[1024]{0:T(1024)S(1)} %bitcast.231, f32[1024]{0:T(1024)S(1)} %bitcast.225, ...), kind=kOutput, calls=%fused_computation.14.clone.1 | convolution fusion | flops 839909376 | bytes 17348096 | tf_op jit(solution)/shard_map/while/body/eval_jaxpr/dot_general | solution.py:125
  287.5 12.1 %multiply_multiply_fusion.4 = (f32[1024,1024]{0,1:T(8,128)S(1)}, f32[1024,1024]{0,1:T(8,128)}) fusion(f32[1024,1024]{0,1:T(8,128)} %get-tuple-element.459, s32[1024]{0:T(1024)S(1)} %get-tuple-element.460, f32[1024]{0:T(1024)S(1)} %bitcast.219, f32[1024]{0:T(1024)S(1)} %bitcast.221, f32[1024]{0:T(1024)S(1)} %bitcast.231, f32[1024]{0:T(1024)S(1)} %bitcast.225, ...), kind=kOutput, calls=%fused_computation.14.clone.1 | convolution fusion | flops 839909376 | bytes 17348096 | tf_op jit(solution)/shard_map/while/body/eval_jaxpr/dot_general | solution.py:125
  316.6 12.1 %multiply_multiply_fusion.4 = (f32[1024,1024]{0,1:T(8,128)S(1)}, f32[1024,1024]{0,1:T(8,128)}) fusion(f32[1024,1024]{0,1:T(8,128)} %get-tuple-element.459, s32[1024]{0:T(1024)S(1)} %get-tuple-element.460, f32[1024]{0:T(1024)S(1)} %bitcast.219, f32[1024]{0:T(1024)S(1)} %bitcast.221, f32[1024]{0:T(1024)S(1)} %bitcast.231, f32[1024]{0:T(1024)S(1)} %bitcast.225, ...), kind=kOutput, calls=%fused_computation.14.clone.1 | convolution fusion | flops 839909376 | bytes 17348096 | tf_op jit(solution)/shard_map/while/body/eval_jaxpr/dot_general | solution.py:125
  345.7 12.1 %multiply_multiply_fusion.4 = (f32[1024,1024]{0,1:T(8,128)S(1)}, f32[1024,1024]{0,1:T(8,128)}) fusion(f32[1024,1024]{0,1:T(8,128)} %get-tuple-element.459, s32[1024]{0:T(1024)S(1)} %get-tuple-element.460, f32[1024]{0:T(1024)S(1)} %bitcast.219, f32[1024]{0:T(1024)S(1)} %bitcast.221, f32[1024]{0:T(1024)S(1)} %bitcast.231, f32[1024]{0:T(1024)S(1)} %bitcast.225, ...), kind=kOutput, calls=%fused_computation.14.clone.1 | convolution fusion | flops 839909376 | bytes 17348096 | tf_op jit(solution)/shard_map/while/body/eval_jaxpr/dot_general | solution.py:125
  374.8 12.1 %multiply_multiply_fusion.4 = (f32[1024,1024]{0,1:T(8,128)S(1)}, f32[1024,1024]{0,1:T(8,128)}) fusion(f32[1024,1024]{0,1:T(8,128)} %get-tuple-element.459, s32[1024]{0:T(1024)S(1)} %get-tuple-element.460, f32[1024]{0:T(1024)S(1)} %bitcast.219, f32[1024]{0:T(1024)S(1)} %bitcast.221, f32[1024]{0:T(1024)S(1)} %bitcast.231, f32[1024]{0:T(1024)S(1)} %bitcast.225, ...), kind=kOutput, calls=%fused_computation.14.clone.1 | convolution fusion | flops 839909376 | bytes 17348096 | tf_op jit(solution)/shard_map/while/body/eval_jaxpr/dot_general | solution.py:125
  403.9 12.1 %multiply_multiply_fusion.4 = (f32[1024,1024]{0,1:T(8,128)S(1)}, f32[1024,1024]{0,1:T(8,128)}) fusion(f32[1024,1024]{0,1:T(8,128)} %get-tuple-element.459, s32[1024]{0:T(1024)S(1)} %get-tuple-element.460, f32[1024]{0:T(1024)S(1)} %bitcast.219, f32[1024]{0:T(1024)S(1)} %bitcast.221, f32[1024]{0:T(1024)S(1)} %bitcast.231, f32[1024]{0:T(1024)S(1)} %bitcast.225, ...), kind=kOutput, calls=%fused_computation.14.clone.1 | convolution fusion | flops 839909376 | bytes 17348096 | tf_op jit(solution)/shard_map/while/body/eval_jaxpr/dot_general | solution.py:125
  433.0 12.1 %multiply_multiply_fusion.4 = (f32[1024,1024]{0,1:T(8,128)S(1)}, f32[1024,1024]{0,1:T(8,128)}) fusion(f32[1024,1024]{0,1:T(8,128)} %get-tuple-element.459, s32[1024]{0:T(1024)S(1)} %get-tuple-element.460, f32[1024]{0:T(1024)S(1)} %bitcast.219, f32[1024]{0:T(1024)S(1)} %bitcast.221, f32[1024]{0:T(1024)S(1)} %bitcast.231, f32[1024]{0:T(1024)S(1)} %bitcast.225, ...), kind=kOutput, calls=%fused_computation.14.clone.1 | convolution fusion | flops 839909376 | bytes 17348096 | tf_op jit(solution)/shard_map/while/body/eval_jaxpr/dot_general | solution.py:125
  462.1 12.1 %multiply_multiply_fusion.4 = (f32[1024,1024]{0,1:T(8,128)S(1)}, f32[1024,1024]{0,1:T(8,128)}) fusion(f32[1024,1024]{0,1:T(8,128)} %get-tuple-element.459, s32[1024]{0:T(1024)S(1)} %get-tuple-element.460, f32[1024]{0:T(1024)S(1)} %bitcast.219, f32[1024]{0:T(1024)S(1)} %bitcast.221, f32[1024]{0:T(1024)S(1)} %bitcast.231, f32[1024]{0:T(1024)S(1)} %bitcast.225, ...), kind=kOutput, calls=%fused_computation.14.clone.1 | convolution fusion | flops 839909376 | bytes 17348096 | tf_op jit(solution)/shard_map/while/body/eval_jaxpr/dot_general | solution.py:125
  491.2 12.1 %multiply_multiply_fusion.4 = (f32[1024,1024]{0,1:T(8,128)S(1)}, f32[1024,1024]{0,1:T(8,128)}) fusion(f32[1024,1024]{0,1:T(8,128)} %get-tuple-element.459, s32[1024]{0:T(1024)S(1)} %get-tuple-element.460, f32[1024]{0:T(1024)S(1)} %bitcast.219, f32[1024]{0:T(1024)S(1)} %bitcast.221, f32[1024]{0:T(1024)S(1)} %bitcast.231, f32[1024]{0:T(1024)S(1)} %bitcast.225, ...), kind=kOutput, calls=%fused_computation.14.clone.1 | convolution fusion | flops 839909376 | bytes 17348096 | tf_op jit(solution)/shard_map/while/body/eval_jaxpr/dot_general | solution.py:125
  520.3 12.1 %multiply_multiply_fusion.4 = (f32[1024,1024]{0,1:T(8,128)S(1)}, f32[1024,1024]{0,1:T(8,128)}) fusion(f32[1024,1024]{0,1:T(8,128)} %get-tuple-element.459, s32[1024]{0:T(1024)S(1)} %get-tuple-element.460, f32[1024]{0:T(1024)S(1)} %bitcast.219, f32[1024]{0:T(1024)S(1)} %bitcast.221, f32[1024]{0:T(1024)S(1)} %bitcast.231, f32[1024]{0:T(1024)S(1)} %bitcast.225, ...), kind=kOutput, calls=%fused_computation.14.clone.1 | convolution fusion | flops 839909376 | bytes 17348096 | tf_op jit(solution)/shard_map/while/body/eval_jaxpr/dot_general | solution.py:125
  549.4 12.1 %multiply_multiply_fusion.4 = (f32[1024,1024]{0,1:T(8,128)S(1)}, f32[1024,1024]{0,1:T(8,128)}) fusion(f32[1024,1024]{0,1:T(8,128)} %get-tuple-element.459, s32[1024]{0:T(1024)S(1)} %get-tuple-element.460, f32[1024]{0:T(1024)S(1)} %bitcast.219, f32[1024]{0:T(1024)S(1)} %bitcast.221, f32[1024]{0:T(1024)S(1)} %bitcast.231, f32[1024]{0:T(1024)S(1)} %bitcast.225, ...), kind=kOutput, calls=%fused_computation.14.clone.1 | convolution fusion | flops 839909376 | bytes 17348096 | tf_op jit(solution)/shard_map/while/body/eval_jaxpr/dot_general | solution.py:125
  578.5 12.1 %multiply_multiply_fusion.4 = (f32[1024,1024]{0,1:T(8,128)S(1)}, f32[1024,1024]{0,1:T(8,128)}) fusion(f32[1024,1024]{0,1:T(8,128)} %get-tuple-element.459, s32[1024]{0:T(1024)S(1)} %get-tuple-element.460, f32[1024]{0:T(1024)S(1)} %bitcast.219, f32[1024]{0:T(1024)S(1)} %bitcast.221, f32[1024]{0:T(1024)S(1)} %bitcast.231, f32[1024]{0:T(1024)S(1)} %bitcast.225, ...), kind=kOutput, calls=%fused_computation.14.clone.1 | convolution fusion | flops 839909376 | bytes 17348096 | tf_op jit(solution)/shard_map/while/body/eval_jaxpr/dot_general | solution.py:125
  607.6 12.1 %multiply_multiply_fusion.4 = (f32[1024,1024]{0,1:T(8,128)S(1)}, f32[1024,1024]{0,1:T(8,128)}) fusion(f32[1024,1024]{0,1:T(8,128)} %get-tuple-element.459, s32[1024]{0:T(1024)S(1)} %get-tuple-element.460, f32[1024]{0:T(1024)S(1)} %bitcast.219, f32[1024]{0:T(1024)S(1)} %bitcast.221, f32[1024]{0:T(1024)S(1)} %bitcast.231, f32[1024]{0:T(1024)S(1)} %bitcast.225, ...), kind=kOutput, calls=%fused_computation.14.clone.1 | convolution fusion | flops 839909376 | bytes 17348096 | tf_op jit(solution)/shard_map/while/body/eval_jaxpr/dot_general | solution.py:125
  636.8 22.2 %fusion.53 = f32[1024,128]{1,0:T(8,128)S(1)} fusion(f32[3,16,128,64]{2,0,3,1:T(4,128)S(1)} %fusion.38, f32[3,1024,16]{1,2,0:T(8,128)} %get-tuple-element.286, f32[1024,16,64]{0,2,1:T(8,128)} %bitcast.204), kind=kOutput, calls=%fused_computation.74 | convolution fusion | flops 4834983936 | bytes 6488064 | tf_op jit(solution)/shard_map/kthp,khnp->tn/dot_general | solution.py:100
  672.7 12.9 %collective-permute-done.4 = f32[1,16,128,64]{2,3,1,0:T(8,128)S(1)} collective-permute-done((f32[1,16,128,64]{2,3,1,0:T(8,128)S(1)}, f32[1,16,128,64]{2,3,1,0:T(8,128)S(1)}, u32[]{:S(2)}, u32[]{:S(2)}) %collective-permute-start.4) | collective-permute-done | bytes 524320 | tf_op jit(solution)/shard_map/ppermute | solution.py:10
  (249 shorter events, 385.9 us)
Async XLA Ops:
  7.2 89.2 %all-gather.4.cloned.1.call-start = ((), (), s32[]{:S(2)}) async-start(), calls=%async_computation.4 | async-start | bytes 4718592 | tf_op jit(solution)/shard_map/all_gather | solution.py:78
  19.9 694.5 %reduce-scatter.5.cloned.1.call-start = ((), (), s32[]{:S(2)}) async-start(), calls=%async_computation.3 | async-start | bytes 655360 | tf_op jit(solution)/shard_map/reduce_scatter | solution.py:159
  22.5 34.3 %collective-permute-start = (f32[]{:T(128)}, f32[]{:T(128)}, u32[]{:S(2)}, u32[]{:S(2)}) collective-permute-start(f32[]{:T(128)} %bitcast.26), channel_id=1, source_target_pairs={{0,4},{4,0},{8,12},{12,8},{16,20},{20,16},{24,28},{28,24},{1,5},{5... | collective-permute-start | bytes 20 | tf_op jit(solution)/shard_map/ppermute | solution.py:10
  52.4 52.2 %copy-start.5 = (f32[1024,128]{1,0:T(8,128)S(1)}, f32[1024,128]{1,0:T(8,128)}, u32[]{:S(2)}) copy-start(f32[1024,128]{1,0:T(8,128)} %param.12) | copy-start | bytes 1572868
  58.1 3.6 collective-permute-start.1
  129.2 35.3 %collective-permute-start.2 = (f32[3,16,128,64]{2,3,1,0:T(8,128)}, f32[3,16,128,64]{2,3,1,0:T(8,128)}, u32[]{:S(2)}, u32[]{:S(2)}) collective-permute-start(f32[3,16,128,64]{2,3,1,0:T(8,128)} %fusion.50), channel_id=1, source_target_pairs={{0,4},{4,0},{8,12},{12,8},{16,20},{20,16},{24,28},{28,24},{1,5},{5... | collective-permute-start | bytes 4718600 | tf_op jit(solution)/shard_map/ppermute | solution.py:10
  168.6 490.4 %collective-permute-start.3 = (f32[2,16,128,64]{2,3,1,0:T(8,128)}, f32[2,16,128,64]{2,3,1,0:T(8,128)}, u32[]{:S(2)}, u32[]{:S(2)}) collective-permute-start(f32[2,16,128,64]{2,3,1,0:T(8,128)} %multiply_add_fusion), channel_id=1, source_target_pairs={{0,8},{4,12},{8,0},{12,4},{16,24},{20,28},{24,16},{28,20},{1,9},{5... | collective-permute-start | bytes 3145736 | tf_op jit(solution)/shard_map/ppermute | solution.py:10
  200.1 12.1 %copy-start.6 = (f32[1024,1024]{0,1:T(8,128)S(1)}, f32[1024,1024]{0,1:T(8,128)}, u32[]{:S(2)}) copy-start(f32[1024,1024]{0,1:T(8,128)} %get-tuple-element.459) | copy-start | bytes 12582916 | tf_op jit(solution)/shard_map/while
  229.2 12.1 %copy-start.6 = (f32[1024,1024]{0,1:T(8,128)S(1)}, f32[1024,1024]{0,1:T(8,128)}, u32[]{:S(2)}) copy-start(f32[1024,1024]{0,1:T(8,128)} %get-tuple-element.459) | copy-start | bytes 12582916 | tf_op jit(solution)/shard_map/while
  258.3 12.1 %copy-start.6 = (f32[1024,1024]{0,1:T(8,128)S(1)}, f32[1024,1024]{0,1:T(8,128)}, u32[]{:S(2)}) copy-start(f32[1024,1024]{0,1:T(8,128)} %get-tuple-element.459) | copy-start | bytes 12582916 | tf_op jit(solution)/shard_map/while
  287.5 12.1 %copy-start.6 = (f32[1024,1024]{0,1:T(8,128)S(1)}, f32[1024,1024]{0,1:T(8,128)}, u32[]{:S(2)}) copy-start(f32[1024,1024]{0,1:T(8,128)} %get-tuple-element.459) | copy-start | bytes 12582916 | tf_op jit(solution)/shard_map/while
  316.6 12.1 %copy-start.6 = (f32[1024,1024]{0,1:T(8,128)S(1)}, f32[1024,1024]{0,1:T(8,128)}, u32[]{:S(2)}) copy-start(f32[1024,1024]{0,1:T(8,128)} %get-tuple-element.459) | copy-start | bytes 12582916 | tf_op jit(solution)/shard_map/while
  345.7 12.1 %copy-start.6 = (f32[1024,1024]{0,1:T(8,128)S(1)}, f32[1024,1024]{0,1:T(8,128)}, u32[]{:S(2)}) copy-start(f32[1024,1024]{0,1:T(8,128)} %get-tuple-element.459) | copy-start | bytes 12582916 | tf_op jit(solution)/shard_map/while
  374.8 12.1 %copy-start.6 = (f32[1024,1024]{0,1:T(8,128)S(1)}, f32[1024,1024]{0,1:T(8,128)}, u32[]{:S(2)}) copy-start(f32[1024,1024]{0,1:T(8,128)} %get-tuple-element.459) | copy-start | bytes 12582916 | tf_op jit(solution)/shard_map/while
  403.9 12.1 %copy-start.6 = (f32[1024,1024]{0,1:T(8,128)S(1)}, f32[1024,1024]{0,1:T(8,128)}, u32[]{:S(2)}) copy-start(f32[1024,1024]{0,1:T(8,128)} %get-tuple-element.459) | copy-start | bytes 12582916 | tf_op jit(solution)/shard_map/while
  433.0 12.1 %copy-start.6 = (f32[1024,1024]{0,1:T(8,128)S(1)}, f32[1024,1024]{0,1:T(8,128)}, u32[]{:S(2)}) copy-start(f32[1024,1024]{0,1:T(8,128)} %get-tuple-element.459) | copy-start | bytes 12582916 | tf_op jit(solution)/shard_map/while
  462.1 12.1 %copy-start.6 = (f32[1024,1024]{0,1:T(8,128)S(1)}, f32[1024,1024]{0,1:T(8,128)}, u32[]{:S(2)}) copy-start(f32[1024,1024]{0,1:T(8,128)} %get-tuple-element.459) | copy-start | bytes 12582916 | tf_op jit(solution)/shard_map/while
  491.2 12.1 %copy-start.6 = (f32[1024,1024]{0,1:T(8,128)S(1)}, f32[1024,1024]{0,1:T(8,128)}, u32[]{:S(2)}) copy-start(f32[1024,1024]{0,1:T(8,128)} %get-tuple-element.459) | copy-start | bytes 12582916 | tf_op jit(solution)/shard_map/while
  520.3 12.1 %copy-start.6 = (f32[1024,1024]{0,1:T(8,128)S(1)}, f32[1024,1024]{0,1:T(8,128)}, u32[]{:S(2)}) copy-start(f32[1024,1024]{0,1:T(8,128)} %get-tuple-element.459) | copy-start | bytes 12582916 | tf_op jit(solution)/shard_map/while
  607.6 12.1 %copy-start.6 = (f32[1024,1024]{0,1:T(8,128)S(1)}, f32[1024,1024]{0,1:T(8,128)}, u32[]{:S(2)}) copy-start(f32[1024,1024]{0,1:T(8,128)} %get-tuple-element.459) | copy-start | bytes 12582916 | tf_op jit(solution)/shard_map/while
  636.8 26.9 %copy-start.3 = (f32[1024,1024]{0,1:T(8,128)S(1)}, f32[1024,1024]{0,1:T(8,128)}, u32[]{:S(2)}) copy-start(f32[1024,1024]{0,1:T(8,128)} %get-tuple-element.96) | copy-start | bytes 12582916
  661.2 24.5 %collective-permute-start.4 = (f32[1,16,128,64]{2,3,1,0:T(8,128)S(1)}, f32[1,16,128,64]{2,3,1,0:T(8,128)S(1)}, u32[]{:S(2)}, u32[]{:S(2)}) collective-permute-start(f32[1,16,128,64]{2,3,1,0:T(8,128)S(1)} %get-tuple-element.285), channel_id=1, source_target_pairs={{0,16},{4,20},{8,24},{12,28},{16,0},{20,4},{24,8},{28,12},{1,17},{... | collective-permute-start | bytes 1572872 | tf_op jit(solution)/shard_map/ppermute | solution.py:10
  671.4 51.1 %reduce-scatter.3.cloned.1.call-start = ((), (), s32[]{:S(2)}) async-start(), calls=%async_computation.2 | async-start | bytes 655360 | tf_op jit(solution)/shard_map/reduce_scatter | solution.py:158
  671.5 18.9 %copy-start.2 = (f32[16,1024,64]{1,2,0:T(8,128)S(1)}, f32[16,1024,64]{1,2,0:T(8,128)}, u32[]{:S(2)}) copy-start(f32[16,1024,64]{1,2,0:T(8,128)} %get-tuple-element.472) | copy-start | bytes 12582916
  (11 other events, 94.5 us)
Sparse Core Ops, SparseCore 0:
  20.0 76.3 all-gather.3
  671.5 19.2 reduce-scatter.4
  701.5 20.9 reduce-scatter.2
where the time goes:
time: 737 us; the launch traced here: 729 us
  matrix products  440 us (60%)
  other arithmetic  91.3 us (12%)
  local copies, waits for them, and re-layouts  75.5 us (10%)
  waiting for transfers between devices  73.7 us (10%)
  blocking collectives  21.2 us (3%)
  between operations  18.3 us (2%)
  starting transfers between devices  8.59 us (1%)
    dot_general x16, matrix products, head_step(): inner = jnp.dot(cot_one, x_one.T, precision=highest)  194 us
    dot_general x16, matrix products, head_step(): grad_x_one = jnp.dot(weighted.T, cot_one, precision=highest)  151 us
    reduce_sum x16, other arithmetic, head_step(): jnp.sum(jnp.where(local_level == level, plain, 0.0), axis=1)  66 us
    all_gather x1, waiting for transfers between devices, local(): lax.all_gather(tail_total[None], 'seq', axis=0, tiled=True)  33.9 us
    ppermute x5, waiting for transfers between devices, from_partner(): lax.ppermute(x, axis, [(i, i ^ 1 << apart) for i in range(lax.axis_size(a...  31.6 us
    dynamic_update_slice x32, local copies, waits for them, and re-layouts, local(): lax.scan(head_step, jnp.zeros((rows_dev, rows_dev), jnp.float32), pieces)  26.7 us
    dot_general x1, matrix products, local(): jnp.einsum('kthp,khnp->tn', weighted_cot, fwd_state, precision=highest)  22.2 us
    unnamed x1, blocking collectives  21.2 us
  transfers between devices with their start and end apart: 8, of which 5 were waited for; matrix products, arithmetic and copies ran while one was open for 76% of the time, Pallas kernels for 0%

commit v1 on v0

--- a/solution.py
+++ b/solution.py
@@ -4,6 +4,18 @@
 from jax.sharding import PartitionSpec as P
 
 STRETCH = 64
+
+
+def doubled_up(array, axis, dim):
+    ways, here = (lax.axis_size(axis), lax.axis_index(axis))
+    grown, reach = (array, 1)
+    while reach < ways:
+        theirs = lax.ppermute(grown, axis, [(d, d ^ reach) for d in range(ways)])
+        mine_first = jnp.concatenate([grown, theirs], axis=dim)
+        theirs_first = jnp.concatenate([theirs, grown], axis=dim)
+        grown = jnp.where(here & reach == 0, mine_first, theirs_first)
+        reach = 2 * reach
+    return grown
 
 
 def from_partner(x, axis, apart):
@@ -75,7 +87,7 @@
         after_clean = (1.0 - upper_half) * far_clean * after_clean + upper_half * after_clean
         own_clean = own_clean * far_clean
     all_tail, all_clean = (
-        lax.all_gather(tail_total[None], "seq", axis=0, tiled=True),
+        doubled_up(tail_total[None], "seq", 0),
         lax.all_gather(device_clean[None], "seq", axis=0, tiled=True),
     )
     zero_count = jnp.cumsum(1.0 - all_clean)

time: 737 us -> 813 us (1.10)
  starting transfers between devices: 8.59 us -> 56.5 us
  blocking collectives: 21.2 us -> 54.2 us
    ppermute x5, starting transfers between devices: 8.47 us -> 48.9 us  [from_partner(): lax.ppermute(x, axis, [(i, i ^ 1 << apart) for i in range(lax.axis_size(a...]
    ppermute x0 -> x3, waiting for transfers between devices: none -> 34.6 us  [doubled_up(): theirs = lax.ppermute(grown, axis, [(d, d ^ reach) for d in range(ways)])]
    all_gather x1 -> x0, waiting for transfers between devices: 33.9 us -> none  [local(): lax.all_gather(tail_total[None], 'seq', axis=0, tiled=True)]
    unnamed x1, blocking collectives: 21.2 us -> 54.2 us
    unnamed x28 -> x30, local copies, waits for them, and re-layouts: 18.1 us -> 18.1 us
  transfers between devices with their start and end apart: 8 -> 10, of which waited for: 5 -> 5; matrix products, arithmetic and copies ran while one was open for 76% -> 69% of each run, Pallas kernels for 0% -> 0%
where the time goes in v1:
time: 813 us; the launch traced here: 806 us
  matrix products  436 us (54%)
  other arithmetic  97 us (12%)
  local copies, waits for them, and re-layouts  75.5 us (9%)
  waiting for transfers between devices  67.5 us (8%)
  starting transfers between devices  56.5 us (7%)
  blocking collectives  54.2 us (7%)
  between operations  18.6 us (2%)
    dot_general x16, matrix products, head_step(): inner = jnp.dot(cot_one, x_one.T, precision=highest)  194 us
    dot_general x16, matrix products, head_step(): grad_x_one = jnp.dot(weighted.T, cot_one, precision=highest)  151 us
    reduce_sum x16, other arithmetic, head_step(): jnp.sum(jnp.where(local_level == level, plain, 0.0), axis=1)  66 us
    unnamed x1, blocking collectives  54.2 us
    ppermute x5, starting transfers between devices, from_partner(): lax.ppermute(x, axis, [(i, i ^ 1 << apart) for i in range(lax.axis_size(a...  48.9 us
    ppermute x3, waiting for transfers between devices, doubled_up(): theirs = lax.ppermute(grown, axis, [(d, d ^ reach) for d in range(ways)])  34.6 us
    dynamic_update_slice x32, local copies, waits for them, and re-layouts, local(): lax.scan(head_step, jnp.zeros((rows_dev, rows_dev), jnp.float32), pieces)  26.7 us
    ppermute x5, waiting for transfers between devices, from_partner(): lax.ppermute(x, axis, [(i, i ^ 1 << apart) for i in range(lax.axis_size(a...  24.1 us
  transfers between devices with their start and end apart: 10, of which 5 were waited for; matrix products, arithmetic and copies ran while one was open for 69% of the time, Pallas kernels for 0%

profile of v1, /device:TPU:0, one launch (start us, length us, event | category | flops | bytes accessed | tf_op | source)
XLA Modules:
  0.0 805.9 jit_solution(14678847195894814159)
XLA Ops:
  21.9 11.9 %collective-permute-done.5 = f32[1,16,128,64]{2,3,1,0:T(8,128)S(1)} collective-permute-done((f32[1,16,128,64]{2,3,1,0:T(8,128)S(1)}, f32[1,16,128,64]{2,3,1,0:T(8,128)S(1)}, u32[]{:S(2)}, u32[]{:S(2)}) %collective-permute-start.5) | collective-permute-done | bytes 524320 | tf_op jit(solution)/shard_map/ppermute | solution.py:13
  35.8 22.6 %collective-permute-done.6 = f32[2,16,128,64]{2,3,1,0:T(8,128)} collective-permute-done((f32[2,16,128,64]{2,3,1,0:T(8,128)S(1)}, f32[2,16,128,64]{2,3,1,0:T(8,128)}, u32[]{:S(2)}, u32[]{:S(2)}) %collective-permute-start.6) | collective-permute-done | bytes 1048608 | tf_op jit(solution)/shard_map/ppermute | solution.py:13
  67.7 54.2 %all-reduce = f32[8]{0:T(128)S(1)} all-reduce(f32[8]{0:T(128)S(1)} %bitcast_dynamic-update-slice_fusion), channel_id=2, replica_groups=mesh['seq'=8,'head'=4] {'seq'}, use_global_device_ids=true, to_apply=%add | all-reduce | flops 8 | bytes 64
  133.3 42.2 %collective-permute-start.1 = (f32[]{:T(128)}, f32[]{:T(128)}, u32[]{:S(2)}, u32[]{:S(2)}) collective-permute-start(f32[]{:T(128)} %mul.366), channel_id=1, source_target_pairs={{0,8},{4,12},{8,0},{12,4},{16,24},{20,28},{24,16},{28,20},{1,9},{5... | collective-permute-start | bytes 20 | tf_op jit(solution)/shard_map/ppermute | solution.py:22
  185.1 11.4 %fusion.30 = f32[3,1024,16]{1,2,0:T(8,128)S(1)} fusion(f32[1024,16,64]{0,2,1:T(8,128)S(1)} %bitcast.203, f32[3,16,128,64]{2,0,3,1:T(4,128)S(1)} %fusion.38, f32[1024,128]{1,0:T(8,128)S(1)} %copy-done.5), kind=kOutput, calls=%fused_computation.50 | convolution fusion | flops 4838080512 | bytes 6488064 | tf_op jit(solution)/shard_map/tn,khnp->kthp/dot_general | solution.py:113
  229.3 13.5 %collective-permute-done.2 = f32[3,16,128,64]{2,3,1,0:T(8,128)} collective-permute-done((f32[3,16,128,64]{2,3,1,0:T(8,128)}, f32[3,16,128,64]{2,3,1,0:T(8,128)}, u32[]{:S(2)}, u32[]{:S(2)}) %collective-permute-start.2) | collective-permute-done | bytes 1572896 | tf_op jit(solution)/shard_map/ppermute | solution.py:22
  248.3 465.9 %while.16 = (s32[]{:T(128)}, f32[1024,1024]{0,1:T(8,128)}, f32[16,1024,64]{1,2,0:T(8,128)}, f32[16,5,1024]{2,0,1:T(8,128)}, f32[16,1024]{1,0:T(8,128)}, /*index=...) while((s32[]{:T(128)}, f32[1024,1024]{0,1:T(8,128)}, ...), condition=%wide.region_7.8_spmd.clone.clone, body=%wide.region_1.7_spmd.clone.clone.sunk | while | flops 1703930880 | bytes 43289372 | solution.py:157
  250.4 11.7 %multiply_multiply_fusion.4 = (f32[1024,1024]{0,1:T(8,128)S(1)}, f32[1024,1024]{0,1:T(8,128)}) fusion(f32[1024,1024]{0,1:T(8,128)} %get-tuple-element.427, s32[1024]{0:T(1024)S(1)} %get-tuple-element.428, f32[1024]{0:T(1024)S(1)} %bitcast.219, f32[1024]{0:T(1024)S(1)} %bitcast.221, f32[1024]{0:T(1024)S(1)} %bitcast.231, f32[1024]{0:T(1024)S(1)} %bitcast.225, ...), kind=kOutput, calls=%fused_computation.14.clone.1 | convolution fusion | flops 839909376 | bytes 17348096 | tf_op jit(solution)/shard_map/while/body/eval_jaxpr/dot_general | solution.py:137
  279.1 12.1 %multiply_multiply_fusion.4 = (f32[1024,1024]{0,1:T(8,128)S(1)}, f32[1024,1024]{0,1:T(8,128)}) fusion(f32[1024,1024]{0,1:T(8,128)} %get-tuple-element.427, s32[1024]{0:T(1024)S(1)} %get-tuple-element.428, f32[1024]{0:T(1024)S(1)} %bitcast.219, f32[1024]{0:T(1024)S(1)} %bitcast.221, f32[1024]{0:T(1024)S(1)} %bitcast.231, f32[1024]{0:T(1024)S(1)} %bitcast.225, ...), kind=kOutput, calls=%fused_computation.14.clone.1 | convolution fusion | flops 839909376 | bytes 17348096 | tf_op jit(solution)/shard_map/while/body/eval_jaxpr/dot_general | solution.py:137
  308.2 12.1 %multiply_multiply_fusion.4 = (f32[1024,1024]{0,1:T(8,128)S(1)}, f32[1024,1024]{0,1:T(8,128)}) fusion(f32[1024,1024]{0,1:T(8,128)} %get-tuple-element.427, s32[1024]{0:T(1024)S(1)} %get-tuple-element.428, f32[1024]{0:T(1024)S(1)} %bitcast.219, f32[1024]{0:T(1024)S(1)} %bitcast.221, f32[1024]{0:T(1024)S(1)} %bitcast.231, f32[1024]{0:T(1024)S(1)} %bitcast.225, ...), kind=kOutput, calls=%fused_computation.14.clone.1 | convolution fusion | flops 839909376 | bytes 17348096 | tf_op jit(solution)/shard_map/while/body/eval_jaxpr/dot_general | solution.py:137
  337.3 12.1 %multiply_multiply_fusion.4 = (f32[1024,1024]{0,1:T(8,128)S(1)}, f32[1024,1024]{0,1:T(8,128)}) fusion(f32[1024,1024]{0,1:T(8,128)} %get-tuple-element.427, s32[1024]{0:T(1024)S(1)} %get-tuple-element.428, f32[1024]{0:T(1024)S(1)} %bitcast.219, f32[1024]{0:T(1024)S(1)} %bitcast.221, f32[1024]{0:T(1024)S(1)} %bitcast.231, f32[1024]{0:T(1024)S(1)} %bitcast.225, ...), kind=kOutput, calls=%fused_computation.14.clone.1 | convolution fusion | flops 839909376 | bytes 17348096 | tf_op jit(solution)/shard_map/while/body/eval_jaxpr/dot_general | solution.py:137
  366.5 12.1 %multiply_multiply_fusion.4 = (f32[1024,1024]{0,1:T(8,128)S(1)}, f32[1024,1024]{0,1:T(8,128)}) fusion(f32[1024,1024]{0,1:T(8,128)} %get-tuple-element.427, s32[1024]{0:T(1024)S(1)} %get-tuple-element.428, f32[1024]{0:T(1024)S(1)} %bitcast.219, f32[1024]{0:T(1024)S(1)} %bitcast.221, f32[1024]{0:T(1024)S(1)} %bitcast.231, f32[1024]{0:T(1024)S(1)} %bitcast.225, ...), kind=kOutput, calls=%fused_computation.14.clone.1 | convolution fusion | flops 839909376 | bytes 17348096 | tf_op jit(solution)/shard_map/while/body/eval_jaxpr/dot_general | solution.py:137
  395.6 12.1 %multiply_multiply_fusion.4 = (f32[1024,1024]{0,1:T(8,128)S(1)}, f32[1024,1024]{0,1:T(8,128)}) fusion(f32[1024,1024]{0,1:T(8,128)} %get-tuple-element.427, s32[1024]{0:T(1024)S(1)} %get-tuple-element.428, f32[1024]{0:T(1024)S(1)} %bitcast.219, f32[1024]{0:T(1024)S(1)} %bitcast.221, f32[1024]{0:T(1024)S(1)} %bitcast.231, f32[1024]{0:T(1024)S(1)} %bitcast.225, ...), kind=kOutput, calls=%fused_computation.14.clone.1 | convolution fusion | flops 839909376 | bytes 17348096 | tf_op jit(solution)/shard_map/while/body/eval_jaxpr/dot_general | solution.py:137
  424.7 12.1 %multiply_multiply_fusion.4 = (f32[1024,1024]{0,1:T(8,128)S(1)}, f32[1024,1024]{0,1:T(8,128)}) fusion(f32[1024,1024]{0,1:T(8,128)} %get-tuple-element.427, s32[1024]{0:T(1024)S(1)} %get-tuple-element.428, f32[1024]{0:T(1024)S(1)} %bitcast.219, f32[1024]{0:T(1024)S(1)} %bitcast.221, f32[1024]{0:T(1024)S(1)} %bitcast.231, f32[1024]{0:T(1024)S(1)} %bitcast.225, ...), kind=kOutput, calls=%fused_computation.14.clone.1 | convolution fusion | flops 839909376 | bytes 17348096 | tf_op jit(solution)/shard_map/while/body/eval_jaxpr/dot_general | solution.py:137
  453.8 12.1 %multiply_multiply_fusion.4 = (f32[1024,1024]{0,1:T(8,128)S(1)}, f32[1024,1024]{0,1:T(8,128)}) fusion(f32[1024,1024]{0,1:T(8,128)} %get-tuple-element.427, s32[1024]{0:T(1024)S(1)} %get-tuple-element.428, f32[1024]{0:T(1024)S(1)} %bitcast.219, f32[1024]{0:T(1024)S(1)} %bitcast.221, f32[1024]{0:T(1024)S(1)} %bitcast.231, f32[1024]{0:T(1024)S(1)} %bitcast.225, ...), kind=kOutput, calls=%fused_computation.14.clone.1 | convolution fusion | flops 839909376 | bytes 17348096 | tf_op jit(solution)/shard_map/while/body/eval_jaxpr/dot_general | solution.py:137
  482.9 12.1 %multiply_multiply_fusion.4 = (f32[1024,1024]{0,1:T(8,128)S(1)}, f32[1024,1024]{0,1:T(8,128)}) fusion(f32[1024,1024]{0,1:T(8,128)} %get-tuple-element.427, s32[1024]{0:T(1024)S(1)} %get-tuple-element.428, f32[1024]{0:T(1024)S(1)} %bitcast.219, f32[1024]{0:T(1024)S(1)} %bitcast.221, f32[1024]{0:T(1024)S(1)} %bitcast.231, f32[1024]{0:T(1024)S(1)} %bitcast.225, ...), kind=kOutput, calls=%fused_computation.14.clone.1 | convolution fusion | flops 839909376 | bytes 17348096 | tf_op jit(solution)/shard_map/while/body/eval_jaxpr/dot_general | solution.py:137
  512.0 12.1 %multiply_multiply_fusion.4 = (f32[1024,1024]{0,1:T(8,128)S(1)}, f32[1024,1024]{0,1:T(8,128)}) fusion(f32[1024,1024]{0,1:T(8,128)} %get-tuple-element.427, s32[1024]{0:T(1024)S(1)} %get-tuple-element.428, f32[1024]{0:T(1024)S(1)} %bitcast.219, f32[1024]{0:T(1024)S(1)} %bitcast.221, f32[1024]{0:T(1024)S(1)} %bitcast.231, f32[1024]{0:T(1024)S(1)} %bitcast.225, ...), kind=kOutput, calls=%fused_computation.14.clone.1 | convolution fusion | flops 839909376 | bytes 17348096 | tf_op jit(solution)/shard_map/while/body/eval_jaxpr/dot_general | solution.py:137
  541.1 12.1 %multiply_multiply_fusion.4 = (f32[1024,1024]{0,1:T(8,128)S(1)}, f32[1024,1024]{0,1:T(8,128)}) fusion(f32[1024,1024]{0,1:T(8,128)} %get-tuple-element.427, s32[1024]{0:T(1024)S(1)} %get-tuple-element.428, f32[1024]{0:T(1024)S(1)} %bitcast.219, f32[1024]{0:T(1024)S(1)} %bitcast.221, f32[1024]{0:T(1024)S(1)} %bitcast.231, f32[1024]{0:T(1024)S(1)} %bitcast.225, ...), kind=kOutput, calls=%fused_computation.14.clone.1 | convolution fusion | flops 839909376 | bytes 17348096 | tf_op jit(solution)/shard_map/while/body/eval_jaxpr/dot_general | solution.py:137
  570.2 12.1 %multiply_multiply_fusion.4 = (f32[1024,1024]{0,1:T(8,128)S(1)}, f32[1024,1024]{0,1:T(8,128)}) fusion(f32[1024,1024]{0,1:T(8,128)} %get-tuple-element.427, s32[1024]{0:T(1024)S(1)} %get-tuple-element.428, f32[1024]{0:T(1024)S(1)} %bitcast.219, f32[1024]{0:T(1024)S(1)} %bitcast.221, f32[1024]{0:T(1024)S(1)} %bitcast.231, f32[1024]{0:T(1024)S(1)} %bitcast.225, ...), kind=kOutput, calls=%fused_computation.14.clone.1 | convolution fusion | flops 839909376 | bytes 17348096 | tf_op jit(solution)/shard_map/while/body/eval_jaxpr/dot_general | solution.py:137
  599.3 12.1 %multiply_multiply_fusion.4 = (f32[1024,1024]{0,1:T(8,128)S(1)}, f32[1024,1024]{0,1:T(8,128)}) fusion(f32[1024,1024]{0,1:T(8,128)} %get-tuple-element.427, s32[1024]{0:T(1024)S(1)} %get-tuple-element.428, f32[1024]{0:T(1024)S(1)} %bitcast.219, f32[1024]{0:T(1024)S(1)} %bitcast.221, f32[1024]{0:T(1024)S(1)} %bitcast.231, f32[1024]{0:T(1024)S(1)} %bitcast.225, ...), kind=kOutput, calls=%fused_computation.14.clone.1 | convolution fusion | flops 839909376 | bytes 17348096 | tf_op jit(solution)/shard_map/while/body/eval_jaxpr/dot_general | solution.py:137
  628.4 12.1 %multiply_multiply_fusion.4 = (f32[1024,1024]{0,1:T(8,128)S(1)}, f32[1024,1024]{0,1:T(8,128)}) fusion(f32[1024,1024]{0,1:T(8,128)} %get-tuple-element.427, s32[1024]{0:T(1024)S(1)} %get-tuple-element.428, f32[1024]{0:T(1024)S(1)} %bitcast.219, f32[1024]{0:T(1024)S(1)} %bitcast.221, f32[1024]{0:T(1024)S(1)} %bitcast.231, f32[1024]{0:T(1024)S(1)} %bitcast.225, ...), kind=kOutput, calls=%fused_computation.14.clone.1 | convolution fusion | flops 839909376 | bytes 17348096 | tf_op jit(solution)/shard_map/while/body/eval_jaxpr/dot_general | solution.py:137
  657.5 12.1 %multiply_multiply_fusion.4 = (f32[1024,1024]{0,1:T(8,128)S(1)}, f32[1024,1024]{0,1:T(8,128)}) fusion(f32[1024,1024]{0,1:T(8,128)} %get-tuple-element.427, s32[1024]{0:T(1024)S(1)} %get-tuple-element.428, f32[1024]{0:T(1024)S(1)} %bitcast.219, f32[1024]{0:T(1024)S(1)} %bitcast.221, f32[1024]{0:T(1024)S(1)} %bitcast.231, f32[1024]{0:T(1024)S(1)} %bitcast.225, ...), kind=kOutput, calls=%fused_computation.14.clone.1 | convolution fusion | flops 839909376 | bytes 17348096 | tf_op jit(solution)/shard_map/while/body/eval_jaxpr/dot_general | solution.py:137
  686.6 12.1 %multiply_multiply_fusion.4 = (f32[1024,1024]{0,1:T(8,128)S(1)}, f32[1024,1024]{0,1:T(8,128)}) fusion(f32[1024,1024]{0,1:T(8,128)} %get-tuple-element.427, s32[1024]{0:T(1024)S(1)} %get-tuple-element.428, f32[1024]{0:T(1024)S(1)} %bitcast.219, f32[1024]{0:T(1024)S(1)} %bitcast.221, f32[1024]{0:T(1024)S(1)} %bitcast.231, f32[1024]{0:T(1024)S(1)} %bitcast.225, ...), kind=kOutput, calls=%fused_computation.14.clone.1 | convolution fusion | flops 839909376 | bytes 17348096 | tf_op jit(solution)/shard_map/while/body/eval_jaxpr/dot_general | solution.py:137
  715.6 22.4 %fusion.53 = f32[1024,128]{1,0:T(8,128)S(1)} fusion(f32[3,16,128,64]{2,0,3,1:T(4,128)S(1)} %fusion.38, f32[3,1024,16]{1,2,0:T(8,128)} %get-tuple-element.254, f32[1024,16,64]{0,2,1:T(8,128)} %bitcast.205), kind=kOutput, calls=%fused_computation.76 | convolution fusion | flops 4834983936 | bytes 6488064 | tf_op jit(solution)/shard_map/kthp,khnp->tn/dot_general | solution.py:112
  (257 shorter events, 414.1 us)
Async XLA Ops:
  7.2 782.9 %reduce-scatter.5.cloned.1.call-start = ((), (), s32[]{:S(2)}) async-start(), calls=%async_computation.3 | async-start | bytes 655360 | tf_op jit(solution)/shard_map/reduce_scatter | solution.py:171
  18.9 45.4 %copy-start.12 = (u32[32]{0:T(128)S(1)}, u32[32]{0:T(128)}, u32[]{:S(2)}) copy-start(u32[32]{0:T(128)} %constant.177) | copy-start | bytes 388
  18.9 14.9 %collective-permute-start.5 = (f32[1,16,128,64]{2,3,1,0:T(8,128)S(1)}, f32[1,16,128,64]{2,3,1,0:T(8,128)S(1)}, u32[]{:S(2)}, u32[]{:S(2)}) collective-permute-start(f32[1,16,128,64]{2,3,1,0:T(8,128)S(1)} %fusion.61), channel_id=1, source_target_pairs={{0,4},{4,0},{8,12},{12,8},{16,20},{20,16},{24,28},{28,24},{1,5},{5... | collective-permute-start | bytes 1572872 | tf_op jit(solution)/shard_map/ppermute | solution.py:13
  33.9 24.5 %collective-permute-start.6 = (f32[2,16,128,64]{2,3,1,0:T(8,128)S(1)}, f32[2,16,128,64]{2,3,1,0:T(8,128)}, u32[]{:S(2)}, u32[]{:S(2)}) collective-permute-start(f32[2,16,128,64]{2,3,1,0:T(8,128)S(1)} %maximum_select_fusion.2), channel_id=1, source_target_pairs={{0,8},{4,12},{8,0},{12,4},{16,24},{20,28},{24,16},{28,20},{1,9},{5... | collective-permute-start | bytes 3145736 | tf_op jit(solution)/shard_map/ppermute | solution.py:13
  61.0 115.9 %collective-permute-start.7 = (f32[4,16,128,64]{2,3,1,0:T(8,128)S(1)}, f32[4,16,128,64]{2,3,1,0:T(8,128)}, u32[]{:S(2)}, u32[]{:S(2)}) collective-permute-start(f32[4,16,128,64]{2,3,1,0:T(8,128)S(1)} %maximum_select_fusion.1), channel_id=1, source_target_pairs={{0,16},{4,20},{8,24},{12,28},{16,0},{20,4},{24,8},{28,12},{1,17},{... | collective-permute-start | bytes 6291464 | tf_op jit(solution)/shard_map/ppermute | solution.py:13
  66.2 65.9 %collective-permute-start = (f32[]{:T(128)}, f32[]{:T(128)}, u32[]{:S(2)}, u32[]{:S(2)}) collective-permute-start(f32[]{:T(128)} %bitcast.26), channel_id=1, source_target_pairs={{0,4},{4,0},{8,12},{12,8},{16,20},{20,16},{24,28},{28,24},{1,5},{5... | collective-permute-start | bytes 20 | tf_op jit(solution)/shard_map/ppermute | solution.py:22
  133.3 42.9 %collective-permute-start.1 = (f32[]{:T(128)}, f32[]{:T(128)}, u32[]{:S(2)}, u32[]{:S(2)}) collective-permute-start(f32[]{:T(128)} %mul.366), channel_id=1, source_target_pairs={{0,8},{4,12},{8,0},{12,4},{16,24},{20,28},{24,16},{28,20},{1,9},{5... | collective-permute-start | bytes 20 | tf_op jit(solution)/shard_map/ppermute | solution.py:22
  209.5 33.3 %collective-permute-start.2 = (f32[3,16,128,64]{2,3,1,0:T(8,128)}, f32[3,16,128,64]{2,3,1,0:T(8,128)}, u32[]{:S(2)}, u32[]{:S(2)}) collective-permute-start(f32[3,16,128,64]{2,3,1,0:T(8,128)} %fusion.50), channel_id=1, source_target_pairs={{0,4},{4,0},{8,12},{12,8},{16,20},{20,16},{24,28},{28,24},{1,5},{5... | collective-permute-start | bytes 4718600 | tf_op jit(solution)/shard_map/ppermute | solution.py:22
  247.0 491.1 %collective-permute-start.3 = (f32[2,16,128,64]{2,3,1,0:T(8,128)}, f32[2,16,128,64]{2,3,1,0:T(8,128)}, u32[]{:S(2)}, u32[]{:S(2)}) collective-permute-start(f32[2,16,128,64]{2,3,1,0:T(8,128)} %multiply_add_fusion), channel_id=1, source_target_pairs={{0,8},{4,12},{8,0},{12,4},{16,24},{20,28},{24,16},{28,20},{1,9},{5... | collective-permute-start | bytes 3145736 | tf_op jit(solution)/shard_map/ppermute | solution.py:22
  279.1 12.1 %copy-start.7 = (f32[1024,1024]{0,1:T(8,128)S(1)}, f32[1024,1024]{0,1:T(8,128)}, u32[]{:S(2)}) copy-start(f32[1024,1024]{0,1:T(8,128)} %get-tuple-element.427) | copy-start | bytes 12582916 | tf_op jit(solution)/shard_map/while
  308.2 12.1 %copy-start.7 = (f32[1024,1024]{0,1:T(8,128)S(1)}, f32[1024,1024]{0,1:T(8,128)}, u32[]{:S(2)}) copy-start(f32[1024,1024]{0,1:T(8,128)} %get-tuple-element.427) | copy-start | bytes 12582916 | tf_op jit(solution)/shard_map/while
  337.3 12.1 %copy-start.7 = (f32[1024,1024]{0,1:T(8,128)S(1)}, f32[1024,1024]{0,1:T(8,128)}, u32[]{:S(2)}) copy-start(f32[1024,1024]{0,1:T(8,128)} %get-tuple-element.427) | copy-start | bytes 12582916 | tf_op jit(solution)/shard_map/while
  366.5 12.1 %copy-start.7 = (f32[1024,1024]{0,1:T(8,128)S(1)}, f32[1024,1024]{0,1:T(8,128)}, u32[]{:S(2)}) copy-start(f32[1024,1024]{0,1:T(8,128)} %get-tuple-element.427) | copy-start | bytes 12582916 | tf_op jit(solution)/shard_map/while
  395.6 12.1 %copy-start.7 = (f32[1024,1024]{0,1:T(8,128)S(1)}, f32[1024,1024]{0,1:T(8,128)}, u32[]{:S(2)}) copy-start(f32[1024,1024]{0,1:T(8,128)} %get-tuple-element.427) | copy-start | bytes 12582916 | tf_op jit(solution)/shard_map/while
  424.7 12.1 %copy-start.7 = (f32[1024,1024]{0,1:T(8,128)S(1)}, f32[1024,1024]{0,1:T(8,128)}, u32[]{:S(2)}) copy-start(f32[1024,1024]{0,1:T(8,128)} %get-tuple-element.427) | copy-start | bytes 12582916 | tf_op jit(solution)/shard_map/while
  453.8 12.1 %copy-start.7 = (f32[1024,1024]{0,1:T(8,128)S(1)}, f32[1024,1024]{0,1:T(8,128)}, u32[]{:S(2)}) copy-start(f32[1024,1024]{0,1:T(8,128)} %get-tuple-element.427) | copy-start | bytes 12582916 | tf_op jit(solution)/shard_map/while
  482.9 12.1 %copy-start.7 = (f32[1024,1024]{0,1:T(8,128)S(1)}, f32[1024,1024]{0,1:T(8,128)}, u32[]{:S(2)}) copy-start(f32[1024,1024]{0,1:T(8,128)} %get-tuple-element.427) | copy-start | bytes 12582916 | tf_op jit(solution)/shard_map/while
  541.1 12.1 %copy-start.7 = (f32[1024,1024]{0,1:T(8,128)S(1)}, f32[1024,1024]{0,1:T(8,128)}, u32[]{:S(2)}) copy-start(f32[1024,1024]{0,1:T(8,128)} %get-tuple-element.427) | copy-start | bytes 12582916 | tf_op jit(solution)/shard_map/while
  570.2 12.1 %copy-start.7 = (f32[1024,1024]{0,1:T(8,128)S(1)}, f32[1024,1024]{0,1:T(8,128)}, u32[]{:S(2)}) copy-start(f32[1024,1024]{0,1:T(8,128)} %get-tuple-element.427) | copy-start | bytes 12582916 | tf_op jit(solution)/shard_map/while
  686.6 12.1 %copy-start.7 = (f32[1024,1024]{0,1:T(8,128)S(1)}, f32[1024,1024]{0,1:T(8,128)}, u32[]{:S(2)}) copy-start(f32[1024,1024]{0,1:T(8,128)} %get-tuple-element.427) | copy-start | bytes 12582916 | tf_op jit(solution)/shard_map/while
  715.5 26.3 %copy-start.3 = (f32[1024,1024]{0,1:T(8,128)S(1)}, f32[1024,1024]{0,1:T(8,128)}, u32[]{:S(2)}) copy-start(f32[1024,1024]{0,1:T(8,128)} %get-tuple-element.96) | copy-start | bytes 12582916
  740.2 21.2 %collective-permute-start.4 = (f32[1,16,128,64]{2,3,1,0:T(8,128)S(1)}, f32[1,16,128,64]{2,3,1,0:T(8,128)S(1)}, u32[]{:S(2)}, u32[]{:S(2)}) collective-permute-start(f32[1,16,128,64]{2,3,1,0:T(8,128)S(1)} %get-tuple-element.253), channel_id=1, source_target_pairs={{0,16},{4,20},{8,24},{12,28},{16,0},{20,4},{24,8},{28,12},{1,17},{... | collective-permute-start | bytes 1572872 | tf_op jit(solution)/shard_map/ppermute | solution.py:22
  749.5 49.4 %reduce-scatter.3.cloned.1.call-start = ((), (), s32[]{:S(2)}) async-start(), calls=%async_computation.2 | async-start | bytes 655360 | tf_op jit(solution)/shard_map/reduce_scatter | solution.py:170
  749.5 16.5 %copy-start.2 = (f32[16,1024,64]{1,2,0:T(8,128)S(1)}, f32[16,1024,64]{1,2,0:T(8,128)}, u32[]{:S(2)}) copy-start(f32[16,1024,64]{1,2,0:T(8,128)} %get-tuple-element.439) | copy-start | bytes 12582916
  (14 other events, 114.9 us)
Sparse Core Ops, SparseCore 0:
  749.6 21.0 reduce-scatter.4
  777.2 21.6 reduce-scatter.2
